TPU v7x, 1024 devices: a whole 8x8x8 slice. The times are simulated.
1024 devices in a mesh: group: 16 (over z, core), ingroup: 64 (over y, x).
Axes of the slice: x: 8, y: 8, z: 8, core: 2. Of those that a mesh axis runs over, the one named last changes fastest.
Arguments:
- tokens: bfloat16 [8192, 3584], P(('group', 'ingroup')), may hold values from -6 to 6
- gate_weight: bfloat16 [1024, 448, 1024], P(('group', 'ingroup')), may hold values from -0.09375 to 0.09375
- up_weight: bfloat16 [1024, 448, 1024], P(('group', 'ingroup')), may hold values from -0.09375 to 0.09375
- hidden_grad: bfloat16 [1024, 512, 128], P(('group', 'ingroup')), may hold values from -6 to 6
- expert_ids: int32 [8192, 8], P(('group', 'ingroup')), may hold values from 0 to 127, as said below
- expert_slot: int32 [8192, 8], P(('group', 'ingroup')), may hold values from -1 to 7, as said below
Outputs:
- token_grad: bfloat16 [8192, 3584], P(('group', 'ingroup'))
Inputs may be any that keep to these rules, and one draw needn't show every extreme that they name: `expert_ids`: each row names 8 different experts that lie in exactly 4 different groups, the group of expert e being e // 8. `expert_slot`: entry (t, k) is -1 where token t is not among the first 4 tokens of its device, in token order, that name the group of expert_ids[t, k]. Among the other pairs that name one expert from the tokens of one column (all devices with one ingroup index, in token order), the first 8 get 0, 1, 2 and so on, and the rest -1.
All inputs are finite; a program needn't handle non-finite values.
Results may differ from a plain program's by a relative error of at most 0.0063.
Values may be sent and summed in bfloat16 or wider, within the bound.
A program may use at most 32 MiB of HBM per device.

v0:
```python
import jax
import jax.numpy as jnp
from jax import lax
from jax.sharding import PartitionSpec as P

EXP_GRP = 8
CAP1 = 4
CAP2 = 8


def partner(block, axis, bit):
    count = lax.axis_size(axis)
    route = []
    for low in range(count):
        high = low | 1 << bit
        if high != low and high < count:
            route += [(low, high), (high, low)]
    return lax.ppermute(block, axis, route)


def activation_grads(pre_gate, pre_up, hidden):
    sigmoid_gate = jax.nn.sigmoid(pre_gate)
    gate_grad = (hidden * pre_up * sigmoid_gate * (1.0 + pre_gate * (1.0 - sigmoid_gate))).astype(
        jnp.bfloat16
    )
    up_grad = (hidden * pre_gate * sigmoid_gate).astype(jnp.bfloat16)
    return (gate_grad, up_grad)


def join_halves(mine, other, upper_half):
    return jnp.where(
        upper_half, jnp.concatenate([other, mine], axis=1), jnp.concatenate([mine, other], axis=1)
    )


def shards(tokens, gate_weight, up_weight, hidden_grad, expert_ids, expert_slot):
    groups_count = lax.axis_size("group")
    ingroup_count = lax.axis_size("ingroup")
    shard_count = ingroup_count // EXP_GRP
    shard_bits = shard_count.bit_length() - 1
    token_count, feature_width = tokens.shape
    expert_total = groups_count * EXP_GRP
    position = lax.axis_index("ingroup")
    group_iota = jnp.arange(groups_count, dtype=jnp.int32)
    named_group = jnp.any(
        (expert_ids // EXP_GRP)[:, :, None] == group_iota[None, None, :], axis=1
    ).astype(jnp.int32)
    group_rank = jnp.cumsum(named_group, axis=0) - 1
    group_slot = jnp.where((named_group > 0) & (group_rank < CAP1), group_rank, -1)
    matched = expert_ids[:, :, None] == jnp.arange(expert_total, dtype=jnp.int32)[None, None, :]
    slot_code = jnp.sum(jnp.where(matched, expert_slot[:, :, None] + 1, 0), axis=1) - 1
    slot_code = slot_code.reshape(token_count, groups_count, EXP_GRP)
    place_one = group_slot.T[:, None, :] == jnp.arange(CAP1, dtype=jnp.int32)[None, :, None]
    place_rows = place_one.astype(jnp.bfloat16)
    send_rows = jnp.einsum(
        "gct,td->gcd", place_rows, tokens, preferred_element_type=jnp.float32
    ).astype(jnp.bfloat16)
    send_codes = (
        jnp.sum(
            jnp.where(place_one[:, :, :, None], slot_code.transpose(1, 0, 2)[:, None, :, :] + 1, 0),
            axis=2,
        )
        - 1
    )
    got_rows, got_codes = (
        lax.all_to_all(send_rows, "group", split_axis=0, concat_axis=0, tiled=True),
        lax.all_to_all(send_codes, "group", split_axis=0, concat_axis=0, tiled=True),
    )
    quarter_width = feature_width // shard_count
    group_row_block = got_rows.reshape(-1, shard_count, quarter_width)
    row_codes = got_codes.reshape(-1, EXP_GRP)
    slot_selection = (
        row_codes.T[:, None, :] == jnp.arange(CAP2, dtype=jnp.int32)[None, :, None]
    ).astype(jnp.bfloat16)
    pieces = jnp.einsum(
        "hyf,fbm->hbym", slot_selection, group_row_block, preferred_element_type=jnp.float32
    ).astype(jnp.bfloat16)
    pieces = pieces.reshape(ingroup_count, CAP2, quarter_width)
    slot_rows = lax.all_to_all(pieces, "ingroup", split_axis=0, concat_axis=0, tiled=True).reshape(
        -1, quarter_width
    )
    gate_local = gate_weight[0]
    up_local = up_weight[0]
    hidden_local = hidden_grad[0].astype(jnp.float32)
    own_width = hidden_local.shape[1]
    gate_part = jnp.dot(slot_rows, gate_local, preferred_element_type=jnp.float32)
    up_part = jnp.dot(slot_rows, up_local, preferred_element_type=jnp.float32)
    for bit_index in range(shard_bits):
        other_gate, other_up = partner((gate_part, up_part), "ingroup", bit_index)
        gate_part = gate_part + other_gate
        up_part = up_part + other_up
    own_start = position % shard_count * own_width
    gate_part = lax.dynamic_slice_in_dim(gate_part, own_start, own_width, 1)
    up_part = lax.dynamic_slice_in_dim(up_part, own_start, own_width, 1)
    gate_grad, up_grad = activation_grads(gate_part, up_part, hidden_local)
    for bit_index in range(shard_bits):
        other_gate, other_up = partner((gate_grad, up_grad), "ingroup", bit_index)
        upper_half = position // 2**bit_index % 2 == 1
        gate_grad = join_halves(gate_grad, other_gate, upper_half)
        up_grad = join_halves(up_grad, other_up, upper_half)
    contract = (((1,), (1,)), ((), ()))
    slot_grad = lax.dot_general(gate_grad, gate_local, contract, preferred_element_type=jnp.float32)
    slot_grad = slot_grad + lax.dot_general(
        up_grad, up_local, contract, preferred_element_type=jnp.float32
    )
    slot_grad = slot_grad.astype(jnp.bfloat16).reshape(ingroup_count, CAP2, quarter_width)
    returned_rows = lax.all_to_all(slot_grad, "ingroup", split_axis=0, concat_axis=0, tiled=True)
    returned_rows = returned_rows.reshape(EXP_GRP, shard_count, CAP2, quarter_width)
    group_sums = jnp.einsum(
        "zpl,zgpx->lgx", slot_selection, returned_rows, preferred_element_type=jnp.float32
    )
    group_sums = group_sums.reshape(groups_count, CAP1, feature_width).astype(jnp.bfloat16)
    back_rows = lax.all_to_all(group_sums, "group", split_axis=0, concat_axis=0, tiled=True)
    token_grad = jnp.einsum(
        "gct,gcd->td", place_rows, back_rows, preferred_element_type=jnp.float32
    )
    return token_grad.astype(jnp.bfloat16)


def solution(mesh):
    in_specs = (
        P(("group", "ingroup"), None),
        P(("group", "ingroup"), None, None),
        P(("group", "ingroup"), None, None),
        P(("group", "ingroup"), None, None),
        P(("group", "ingroup"), None),
        P(("group", "ingroup"), None),
    )
    out_specs = P(("group", "ingroup"), None)
    return jax.shard_map(shards, mesh=mesh, in_specs=in_specs, out_specs=out_specs, check_vma=False)
```

profile of v0, /device:TPU:1, one launch (start us, length us, event | category | flops | bytes accessed | tf_op | source)
XLA Modules:
  0.0 725.2 jit_solution(1231111790647030372)
XLA Ops:
  0.0 0.8 add_select_fusion
  0.8 0.1 fusion.34
  0.9 0.7 broadcast_add_fusion.1
  1.6 0.8 select_reduce_fusion.1
  2.4 0.1 add.72
  2.5 0.1 copy.49
  2.6 0.7 copy.50
  3.3 18.2 %all-to-all-start = ((s32[16,4,8]{2,1,0:T(4,128)}), s32[16,4,8]{2,1,0:T(4,128)S(1)}, u32[]{:S(2)}, u32[]{:S(2)}) async-start(s32[16,4,8]{2,1,0:T(4,128)} %copy.50), calls=%async_computation | async-start | bytes 65536 | tf_op jit(solution)/shard_map/all_to_all | solution.py:67
  21.5 1.1 convolution_convert_fusion
  22.6 1.1 copy.51
  23.8 5.1 all-to-all-done
  28.9 3.7 all-to-all-start.1
  32.7 0.1 copy.52
  32.7 15.9 %all-to-all-done.1 = bf16[16,4,3584]{2,1,0:T(4,128)(2,1)S(1)} async-done(((bf16[16,4,3584]{2,1,0:T(4,128)(2,1)}), bf16[16,4,3584]{2,1,0:T(4,128)(2,1)S(1)}, u32[]{:S(2)}, u32[]{:S(2)}) %all-to-all-start.1) | async-done | bytes 458784 | tf_op jit(solution)/shard_map/all_to_all | solution.py:66
  48.6 0.5 reshape.56
  49.2 0.3 fusion.3
  49.5 31.4 %all_to_all.25 = bf16[64,8,448]{2,1,0:T(8,128)(2,1)S(1)} all-to-all(bf16[64,8,448]{2,1,0:T(8,128)(2,1)S(1)} %bitcast.64), channel_id=1, replica_groups=mesh['group'=16,'ingroup'=64] {'ingroup'}, dimensions={0} | all-to-all | bytes 917504 | tf_op jit(solution)/shard_map/all_to_all | solution.py:79
  81.0 0.7 fusion.18
  81.7 3.7 collective-permute-start.3
  85.4 0.7 fusion.21
  86.1 2.0 collective-permute-start
  88.1 43.2 %collective-permute-done.3 = f32[512,1024]{1,0:T(8,128)S(1)} collective-permute-done((f32[512,1024]{1,0:T(8,128)S(1)}, f32[512,1024]{1,0:T(8,128)S(1)}, u32[]{:S(2)}, u32[]{:S(2)}) %collective-permute-start.3) | collective-permute-done | bytes 2097184 | tf_op jit(solution)/shard_map/ppermute | solution.py:18
  131.3 0.6 add.82
  131.8 4.1 collective-permute-start.4
  135.9 81.4 %collective-permute-done = f32[512,1024]{1,0:T(8,128)S(1)} collective-permute-done((f32[512,1024]{1,0:T(8,128)S(1)}, f32[512,1024]{1,0:T(8,128)S(1)}, u32[]{:S(2)}, u32[]{:S(2)}) %collective-permute-start) | collective-permute-done | bytes 2097184 | tf_op jit(solution)/shard_map/ppermute | solution.py:18
  217.3 0.6 add.77
  217.8 1.9 collective-permute-start.1
  219.8 51.0 %collective-permute-done.4 = f32[512,1024]{1,0:T(8,128)S(1)} collective-permute-done((f32[512,1024]{1,0:T(8,128)S(1)}, f32[512,1024]{1,0:T(8,128)S(1)}, u32[]{:S(2)}, u32[]{:S(2)}) %collective-permute-start.4) | collective-permute-done | bytes 2097184 | tf_op jit(solution)/shard_map/ppermute | solution.py:18
  270.7 0.4 add.83
  271.1 0.0 copy-start.3
  271.2 4.3 collective-permute-start.5
  275.5 86.0 %collective-permute-done.1 = f32[512,1024]{1,0:T(8,128)S(1)} collective-permute-done((f32[512,1024]{1,0:T(8,128)S(1)}, f32[512,1024]{1,0:T(8,128)S(1)}, u32[]{:S(2)}, u32[]{:S(2)}) %collective-permute-start.1) | collective-permute-done | bytes 2097184 | tf_op jit(solution)/shard_map/ppermute | solution.py:18
  361.5 1.7 add.78
  363.2 4.2 collective-permute-start.2
  367.4 0.0 collective-permute-done.5
  367.4 134.1 %collective-permute-done.2 = f32[512,1024]{1,0:T(8,128)} collective-permute-done((f32[512,1024]{1,0:T(8,128)}, f32[512,1024]{1,0:T(8,128)}, u32[]{:S(2)}, u32[]{:S(2)}) %collective-permute-start.2) | collective-permute-done | bytes 2097184 | tf_op jit(solution)/shard_map/ppermute | solution.py:18
  501.5 1.3 fusion.29
  502.8 1.9 collective-permute-start.9
  504.7 4.5 collective-permute-done.9
  509.2 0.1 maximum_select_fusion.7
  509.3 1.9 collective-permute-start.10
  511.3 2.7 collective-permute-start.6
  514.0 4.7 collective-permute-done.6
  518.7 0.1 maximum_select_fusion.6
  518.8 5.1 collective-permute-start.7
  523.9 2.0 collective-permute-done.10
  525.9 0.1 maximum_select_fusion.5
  526.0 3.4 collective-permute-start.11
  529.5 30.0 %collective-permute-done.7 = bf16[512,256]{1,0:T(8,128)(2,1)S(1)} collective-permute-done((bf16[512,256]{1,0:T(8,128)(2,1)S(1)}, bf16[512,256]{1,0:T(8,128)(2,1)S(1)}, u32[]{:S(2)}, u32[]{:S(2)}) %collective-permute-start.7) | collective-permute-done | bytes 262176 | tf_op jit(solution)/shard_map/ppermute | solution.py:18
  559.5 0.1 maximum_select_fusion.4
  559.6 2.4 collective-permute-start.8
  562.1 0.0 copy-start.2
  562.1 0.7 fusion.9
  562.8 24.6 %collective-permute-done.8 = bf16[512,512]{1,0:T(8,128)(2,1)} collective-permute-done((bf16[512,512]{1,0:T(8,128)(2,1)S(1)}, bf16[512,512]{1,0:T(8,128)(2,1)}, u32[]{:S(2)}, u32[]{:S(2)}) %collective-permute-start.8) | collective-permute-done | bytes 524320 | tf_op jit(solution)/shard_map/ppermute | solution.py:18
  587.4 1.9 fusion.2
  589.3 1.0 copy.55
  590.3 7.6 %all-to-all-start.3 = ((bf16[64,8,448]{2,1,0:T(8,128)(2,1)}), bf16[64,8,448]{2,1,0:T(8,128)(2,1)S(1)}, u32[]{:S(2)}, u32[]{:S(2)}) async-start(bf16[64,8,448]{2,1,0:T(8,128)(2,1)} %bitcast.16), calls=%async_computation.3 | async-start | bytes 1048576 | tf_op jit(solution)/shard_map/all_to_all | solution.py:107
  598.0 17.5 %all-to-all-done.3 = bf16[64,8,448]{2,1,0:T(8,128)(2,1)S(1)} async-done(((bf16[64,8,448]{2,1,0:T(8,128)(2,1)}), bf16[64,8,448]{2,1,0:T(8,128)(2,1)S(1)}, u32[]{:S(2)}, u32[]{:S(2)}) %all-to-all-start.3) | async-done | bytes 458784 | tf_op jit(solution)/shard_map/all_to_all | solution.py:107
  615.5 0.2 copy.71
  615.7 0.6 reshape.65
  616.2 0.5 fusion
  616.7 0.4 copy.58
  617.1 107.2 %all_to_all.26 = bf16[16,4,3584]{2,1,0:T(4,128)(2,1)S(1)} all-to-all(bf16[16,4,3584]{2,1,0:T(4,128)(2,1)S(1)} %copy.58), channel_id=1, replica_groups=mesh['group'=16,'ingroup'=64] {'group'}, dimensions={0} | all-to-all | bytes 917504 | tf_op jit(solution)/shard_map/all_to_all | solution.py:113
  724.3 0.9 fusion.1
  (15 shorter events, 0.2 us)
Async XLA Ops:
  0.0 85.4 %copy-start = (bf16[1,448,1024]{2,1,0:T(8,128)(2,1)S(1)}, bf16[1,448,1024]{2,1,0:T(8,128)(2,1)}, u32[]{:S(2)}) copy-start(bf16[1,448,1024]{2,1,0:T(8,128)(2,1)} %param.8) | copy-start | bytes 2752516
  3.3 25.6 %all-to-all-start = ((s32[16,4,8]{2,1,0:T(4,128)}), s32[16,4,8]{2,1,0:T(4,128)S(1)}, u32[]{:S(2)}, u32[]{:S(2)}) async-start(s32[16,4,8]{2,1,0:T(4,128)} %copy.50), calls=%async_computation | async-start | bytes 65536 | tf_op jit(solution)/shard_map/all_to_all | solution.py:67
  28.9 19.7 %all-to-all-start.1 = ((bf16[16,4,3584]{2,1,0:T(4,128)(2,1)}), bf16[16,4,3584]{2,1,0:T(4,128)(2,1)S(1)}, u32[]{:S(2)}, u32[]{:S(2)}) async-start(bf16[16,4,3584]{2,1,0:T(4,128)(2,1)} %copy.51), calls=%async_computation.1 | async-start | bytes 917504 | tf_op jit(solution)/shard_map/all_to_all | solution.py:66
  32.6 48.3 %copy-start.1 = (bf16[1,448,1024]{2,1,0:T(8,128)(2,1)S(1)}, bf16[1,448,1024]{2,1,0:T(8,128)(2,1)}, u32[]{:S(2)}) copy-start(bf16[1,448,1024]{2,1,0:T(8,128)(2,1)} %param.7) | copy-start | bytes 2752516
  81.7 49.6 %collective-permute-start.3 = (f32[512,1024]{1,0:T(8,128)S(1)}, f32[512,1024]{1,0:T(8,128)S(1)}, u32[]{:S(2)}, u32[]{:S(2)}) collective-permute-start(f32[512,1024]{1,0:T(8,128)S(1)} %fusion.18), channel_id=1, source_target_pairs={{0,1},{1,0},{2,3},{3,2},{4,5},{5,4},{6,7},{7,6},{8,9},{9,8},{10,11... | collective-permute-start | bytes 6291464 | tf_op jit(solution)/shard_map/ppermute | solution.py:18
  86.1 131.2 %collective-permute-start = (f32[512,1024]{1,0:T(8,128)S(1)}, f32[512,1024]{1,0:T(8,128)S(1)}, u32[]{:S(2)}, u32[]{:S(2)}) collective-permute-start(f32[512,1024]{1,0:T(8,128)S(1)} %fusion.21), channel_id=1, source_target_pairs={{0,1},{1,0},{2,3},{3,2},{4,5},{5,4},{6,7},{7,6},{8,9},{9,8},{10,11... | collective-permute-start | bytes 6291464 | tf_op jit(solution)/shard_map/ppermute | solution.py:18
  131.8 138.9 %collective-permute-start.4 = (f32[512,1024]{1,0:T(8,128)S(1)}, f32[512,1024]{1,0:T(8,128)S(1)}, u32[]{:S(2)}, u32[]{:S(2)}) collective-permute-start(f32[512,1024]{1,0:T(8,128)S(1)} %add.82), channel_id=1, source_target_pairs={{0,2},{2,0},{1,3},{3,1},{4,6},{6,4},{5,7},{7,5},{8,10},{10,8},{9,1... | collective-permute-start | bytes 6291464 | tf_op jit(solution)/shard_map/ppermute | solution.py:18
  217.8 143.6 %collective-permute-start.1 = (f32[512,1024]{1,0:T(8,128)S(1)}, f32[512,1024]{1,0:T(8,128)S(1)}, u32[]{:S(2)}, u32[]{:S(2)}) collective-permute-start(f32[512,1024]{1,0:T(8,128)S(1)} %add.77), channel_id=1, source_target_pairs={{0,2},{2,0},{1,3},{3,1},{4,6},{6,4},{5,7},{7,5},{8,10},{10,8},{9,1... | collective-permute-start | bytes 6291464 | tf_op jit(solution)/shard_map/ppermute | solution.py:18
  271.1 230.4 %copy-start.3 = (bf16[1,512,128]{2,1,0:T(8,128)(2,1)S(1)}, bf16[1,512,128]{2,1,0:T(8,128)(2,1)}, u32[]{:S(2)}) copy-start(bf16[1,512,128]{2,1,0:T(8,128)(2,1)} %param.9) | copy-start | bytes 393220
  271.2 96.3 %collective-permute-start.5 = (f32[512,1024]{1,0:T(8,128)S(1)}, f32[512,1024]{1,0:T(8,128)}, u32[]{:S(2)}, u32[]{:S(2)}) collective-permute-start(f32[512,1024]{1,0:T(8,128)S(1)} %add.83), channel_id=1, source_target_pairs={{0,4},{4,0},{1,5},{5,1},{2,6},{6,2},{3,7},{7,3},{8,12},{12,8},{9,1... | collective-permute-start | bytes 6291464 | tf_op jit(solution)/shard_map/ppermute | solution.py:18
  363.2 138.3 %collective-permute-start.2 = (f32[512,1024]{1,0:T(8,128)}, f32[512,1024]{1,0:T(8,128)}, u32[]{:S(2)}, u32[]{:S(2)}) collective-permute-start(f32[512,1024]{1,0:T(8,128)} %add.78), channel_id=1, source_target_pairs={{0,4},{4,0},{1,5},{5,1},{2,6},{6,2},{3,7},{7,3},{8,12},{12,8},{9,1... | collective-permute-start | bytes 6291464 | tf_op jit(solution)/shard_map/ppermute | solution.py:18
  502.8 6.5 collective-permute-start.9
  509.3 16.6 %collective-permute-start.10 = (bf16[512,256]{1,0:T(8,128)(2,1)S(1)}, bf16[512,256]{1,0:T(8,128)(2,1)S(1)}, u32[]{:S(2)}, u32[]{:S(2)}) collective-permute-start(bf16[512,256]{1,0:T(8,128)(2,1)S(1)} %maximum_select_fusion.7), channel_id=1, source_target_pairs={{0,2},{2,0},{1,3},{3,1},{4,6},{6,4},{5,7},{7,5},{8,10},{10,8},{9,1... | collective-permute-start | bytes 786440 | tf_op jit(solution)/shard_map/ppermute | solution.py:18
  511.3 7.4 %collective-permute-start.6 = (bf16[512,128]{1,0:T(8,128)(2,1)S(1)}, bf16[512,128]{1,0:T(8,128)(2,1)S(1)}, u32[]{:S(2)}, u32[]{:S(2)}) collective-permute-start(bf16[512,128]{1,0:T(8,128)(2,1)S(1)} %get-tuple-element.5), channel_id=1, source_target_pairs={{0,1},{1,0},{2,3},{3,2},{4,5},{5,4},{6,7},{7,6},{8,9},{9,8},{10,11... | collective-permute-start | bytes 393224 | tf_op jit(solution)/shard_map/ppermute | solution.py:18
  518.8 40.7 %collective-permute-start.7 = (bf16[512,256]{1,0:T(8,128)(2,1)S(1)}, bf16[512,256]{1,0:T(8,128)(2,1)S(1)}, u32[]{:S(2)}, u32[]{:S(2)}) collective-permute-start(bf16[512,256]{1,0:T(8,128)(2,1)S(1)} %maximum_select_fusion.6), channel_id=1, source_target_pairs={{0,2},{2,0},{1,3},{3,1},{4,6},{6,4},{5,7},{7,5},{8,10},{10,8},{9,1... | collective-permute-start | bytes 786440 | tf_op jit(solution)/shard_map/ppermute | solution.py:18
  526.0 36.1 %collective-permute-start.11 = (bf16[512,512]{1,0:T(8,128)(2,1)S(1)}, bf16[512,512]{1,0:T(8,128)(2,1)S(1)}, u32[]{:S(2)}, u32[]{:S(2)}) collective-permute-start(bf16[512,512]{1,0:T(8,128)(2,1)S(1)} %maximum_select_fusion.5), channel_id=1, source_target_pairs={{0,4},{4,0},{1,5},{5,1},{2,6},{6,2},{3,7},{7,3},{8,12},{12,8},{9,1... | collective-permute-start | bytes 1572872 | tf_op jit(solution)/shard_map/ppermute | solution.py:18
  559.6 27.8 %collective-permute-start.8 = (bf16[512,512]{1,0:T(8,128)(2,1)S(1)}, bf16[512,512]{1,0:T(8,128)(2,1)}, u32[]{:S(2)}, u32[]{:S(2)}) collective-permute-start(bf16[512,512]{1,0:T(8,128)(2,1)S(1)} %maximum_select_fusion.4), channel_id=1, source_target_pairs={{0,4},{4,0},{1,5},{5,1},{2,6},{6,2},{3,7},{7,3},{8,12},{12,8},{9,1... | collective-permute-start | bytes 1572872 | tf_op jit(solution)/shard_map/ppermute | solution.py:18
  562.1 25.3 %copy-start.2 = (bf16[1,448,1024]{2,1,0:T(8,128)(2,1)S(1)}, bf16[1,448,1024]{2,1,0:T(8,128)(2,1)}, u32[]{:S(2)}) copy-start(bf16[1,448,1024]{2,1,0:T(8,128)(2,1)} %param.7) | copy-start | bytes 2752516
  590.3 25.2 %all-to-all-start.3 = ((bf16[64,8,448]{2,1,0:T(8,128)(2,1)}), bf16[64,8,448]{2,1,0:T(8,128)(2,1)S(1)}, u32[]{:S(2)}, u32[]{:S(2)}) async-start(bf16[64,8,448]{2,1,0:T(8,128)(2,1)} %bitcast.16), calls=%async_computation.3 | async-start | bytes 1048576 | tf_op jit(solution)/shard_map/all_to_all | solution.py:107
where the time goes:
time: 726 us; the launch traced here: 725 us
  waiting for transfers between devices  500 us (69%)
  blocking collectives  139 us (19%)
  starting transfers between devices  67.3 us (9%)
  other arithmetic  7.36 us (1%)
    ppermute x12, waiting for transfers between devices, partner(): return lax.ppermute(block, axis, route)  461 us
    all_to_all x1, blocking collectives, shards(): lax.all_to_all(group_sums, 'group', split_axis=0, concat_axis=0, tiled=True)  107 us
    ppermute x12, starting transfers between devices, partner(): return lax.ppermute(block, axis, route)  37.7 us
    all_to_all x1, blocking collectives, shards(): lax.all_to_all(pieces, 'ingroup', split_axis=0, concat_axis=0, tiled=True)  31.4 us
    all_to_all x1, starting transfers between devices, shards(): lax.all_to_all(send_codes, 'group', split_axis=0, concat_axis=0, tiled=True)  18.2 us
    all_to_all x1, waiting for transfers between devices, shards(): lax.all_to_all(slot_grad, 'ingroup', split_axis=0, concat_axis=0, tiled=T...  17.5 us
    all_to_all x1, waiting for transfers between devices, shards(): lax.all_to_all(send_rows, 'group', split_axis=0, concat_axis=0, tiled=True)  15.9 us
  transfers between devices with their start and end apart: 15, of which 13 were waited for; matrix products, arithmetic and copies ran while one was open for 1% of the time, Pallas kernels for 0%

commit v1 on v0

v1 whole, which is shorter than its diff:
```python
import functools

import jax
import jax.numpy as jnp
from jax import lax
from jax.experimental import pallas as pl
from jax.experimental.pallas import tpu as pltpu
from jax.sharding import PartitionSpec as P

MESH = pl.DeviceIdType.MESH
BF = jnp.bfloat16
F32 = jnp.float32
CORES = 2
EXP_GRP = 8
CAP1 = 4
CAP2 = 8
META = 64
VMEM_BYTES = 48 * 1024 * 1024


def remote(src, dst, send_sem, recv_sem, device):
    return pltpu.make_async_remote_copy(
        src_ref=src,
        dst_ref=dst,
        send_sem=send_sem,
        recv_sem=recv_sem,
        device_id=device,
        device_id_type=MESH,
    )


def offsets(n):
    order = [0]
    for k in range(1, n // 2):
        order += [k, -k]
    return order + [n // 2]


def dot_nt(a, b):
    return lax.dot_general(a, b, (((1,), (1,)), ((), ())), preferred_element_type=F32)


def dot_tn(a, b):
    return lax.dot_general(a, b, (((0,), (0,)), ((), ())), preferred_element_type=F32)


def kernel(
    dims,
    tok,
    wg,
    wu,
    hg,
    out,
    a_buf,
    g_buf,
    s_buf,
    r_buf,
    w2,
    h_buf,
    rs_s,
    rs_r,
    ag,
    acc,
    t_buf,
    u_buf,
    sel_buf,
    gp,
    cx,
    q_buf,
    zb,
    o_buf,
    f_buf,
    w_sem,
    h_sem,
    x1,
    z1,
    c1,
    y1,
    rs_sem,
    ag_sem,
    y2,
    c2,
    z2,
    x2,
):
    NX, NY, NZ = dims
    NG = NZ * CORES
    TD = tok.shape[1]
    DQ = r_buf.shape[3]
    HQ = hg.shape[1]
    LANES = tok.shape[2]
    RG = NX * CAP2
    MC = 2 * RG
    NCH = NY // 2
    half_x = NX // 2
    order = offsets(NY)

    g = lax.axis_index("group")
    p = lax.axis_index("ingroup")
    z, c = lax.div(g, CORES), lax.rem(g, CORES)
    y, x = lax.div(p, NX), lax.rem(p, NX)

    def xat(o):
        return lax.rem(x + (o + NX), NX)

    def yat(o):
        return lax.rem(y + (o + NY), NY)

    def zat(o):
        return lax.rem(z + (o + NZ), NZ)

    def at_x(xx):
        return (g, y * NX + xx)

    def at_y(yy):
        return (g, yy * NX + x)

    def at_z(zz):
        return (zz * CORES + c, p)

    sibling = (z * CORES + (1 - c), p)

    sends = []

    def start(copy):
        copy.start()
        sends.append(copy)

    loads = []
    for d in range(NX):
        for n, w in enumerate((wg, wu)):
            loads.append(
                pltpu.make_async_copy(
                    w.at[:, pl.ds(d * HQ, HQ)],
                    w2.at[d, :, pl.ds(n * HQ, HQ)],
                    w_sem.at[d * 2 + n],
                )
            )
    loads.append(pltpu.make_async_copy(hg, h_buf, h_sem.at[0]))
    for load in loads:
        load.start()

    barrier = pltpu.get_barrier_semaphore()
    peers = [at_x(xat(o)) for o in range(1, NX)]
    peers += [at_y(yat(o)) for o in range(1, NY)]
    peers += [at_z(zat(o)) for o in range(1, NZ)]
    peers += [sibling]
    for peer in peers:
        pl.semaphore_signal(barrier, inc=1, device_id=peer, device_id_type=MESH)
    pl.semaphore_wait(barrier, len(peers))

    for o in range(1, NX):
        xd = xat(o)
        start(remote(tok.at[xd], a_buf.at[x], x1.at[0, o], x1.at[1, o], at_x(xd)))
    a_buf[pl.ds(x, 1)] = tok[pl.ds(x, 1)]
    for o in range(1, NX):
        xs = xat(-o)
        remote(tok.at[xs], a_buf.at[xs], x1.at[0, o], x1.at[1, o], at_x(xs)).wait_recv()

    for o in range(1, NZ):
        zd = zat(o)
        start(remote(a_buf, g_buf.at[:, g], z1.at[0, o], z1.at[1, o], at_z(zd)))
    start(remote(a_buf, g_buf.at[:, g], c1.at[0, 0], c1.at[1, 0], sibling))
    g_buf[:, pl.ds(g, 1)] = a_buf[...].reshape(NX, 1, TD, LANES)
    for o in range(1, NZ):
        gs = zat(-o) * CORES + c
        remote(a_buf, g_buf.at[:, gs], z1.at[0, o], z1.at[1, o], at_z(zat(-o))).wait_recv()
        start(remote(g_buf.at[:, gs], g_buf.at[:, gs], c1.at[0, o], c1.at[1, o], sibling))
    for o in range(NZ):
        gs = zat(-o) * CORES + (1 - c)
        remote(a_buf, g_buf.at[:, gs], c1.at[0, o], c1.at[1, o], sibling).wait_recv()

    pick_row = lax.broadcasted_iota(jnp.int32, (8, 128), 0)
    pick_lane = lax.broadcasted_iota(jnp.int32, (8, 128), 1)
    pick = jnp.where(pick_lane == 64 + pick_row, 8.0, jnp.where(pick_lane == 72 + pick_row, 1.0, 0.0))
    pick = pick.astype(BF)
    code_of = lax.broadcasted_iota(jnp.int32, (NY * CAP2, NG * TD), 0) + g * (NY * CAP2)
    code_of = code_of.astype(F32)
    for xc in range(NX):
        rows = g_buf[xc].reshape(NG * TD, LANES)
        codes = dot_nt(pick, rows[:, LANES - 128 :])
        sel = jnp.zeros(code_of.shape, F32)
        for k in range(8):
            sel = jnp.where(codes[k : k + 1, :] == code_of, 1.0, sel)
        sel = sel.astype(BF)
        sel_buf[xc] = sel
        picked = jnp.dot(sel, rows[:, :DQ], preferred_element_type=F32).astype(BF)
        s_buf[:, xc] = picked.reshape(NY, CAP2, DQ)

    for i in range(1, NY):
        yd = yat(-order[i])
        start(remote(s_buf.at[yd], r_buf.at[i], y1.at[0, i], y1.at[1, i], at_y(yd)))
    r_buf[pl.ds(0, 1)] = s_buf[pl.ds(y, 1)]
    for load in loads:
        load.wait()

    def weights(d):
        return w2[pl.ds(d, 1)].reshape(DQ, 2 * HQ)

    def slot_rows(j):
        return r_buf[2 * j : 2 * j + 2].reshape(MC, DQ)

    def rs_copy(way, k, j):
        rows = pl.ds(j * MC, MC) if k else pl.ds(j * MC + way * RG, RG)
        sign = 1 - 2 * way
        return remote(
            rs_s.at[way, k, rows],
            rs_r.at[way, k, rows],
            rs_sem.at[0, way, k, j],
            rs_sem.at[1, way, k, j],
            at_x(xat(sign)),
        )

    def ag_copy(way, k, j, src):
        rows = pl.ds(j * MC, MC) if k < half_x - 1 else pl.ds(j * MC + way * RG, RG)
        sign = 1 - 2 * way
        return remote(
            ag.at[src, rows],
            ag.at[src, rows],
            ag_sem.at[0, way, k, j],
            ag_sem.at[1, way, k, j],
            at_x(xat(sign)),
        )

    def y_back(i):
        yd = yat(order[i])
        return remote(t_buf.at[i], u_buf.at[y], y2.at[0, i], y2.at[1, i], at_y(yd))

    def rs_stage(k, j):
        if k == 0:
            for i in (2 * j, 2 * j + 1):
                if i:
                    ys = yat(order[i])
                    remote(s_buf.at[ys], r_buf.at[i], y1.at[0, i], y1.at[1, i], at_y(ys)).wait_recv()
        base = j * MC
        lhs = slot_rows(j)
        for way in range(2):
            sign = 1 - 2 * way
            w = weights(xat(sign * (half_x - k)))
            mine = pl.ds(base + way * RG, RG)
            other = pl.ds(base + (1 - way) * RG, RG)
            if k == 0:
                part = lhs[way * RG : way * RG + RG]
                rs_s[way, 0, mine] = jnp.dot(part, w, preferred_element_type=F32).astype(BF)
            else:
                part = jnp.dot(lhs, w, preferred_element_type=F32)
                rs_copy(way, k - 1, j).wait_recv()
                if k == 1:
                    own = part[way * RG : way * RG + RG]
                    rest = part[(1 - way) * RG : (1 - way) * RG + RG]
                    rs_s[way, 1, mine] = (own + rs_r[way, 0, mine].astype(F32)).astype(BF)
                    rs_s[way, 1, other] = rest.astype(BF)
                else:
                    rows = pl.ds(base, MC)
                    rs_s[way, k, rows] = (part + rs_r[way, k - 1, rows].astype(F32)).astype(BF)
            start(rs_copy(way, k, j))

    def act_stage(j):
        rows = pl.ds(j * MC, MC)
        pre = jnp.dot(slot_rows(j), weights(x), preferred_element_type=F32)
        for way in range(2):
            rs_copy(way, half_x - 1, j).wait_recv()
            pre = pre + rs_r[way, half_x - 1, rows].astype(F32)
        pre_gate, pre_up = pre[:, :HQ], pre[:, HQ:]
        hidden = jnp.concatenate(
            [
                h_buf[pl.ds(yat(order[i]) * RG, RG)].astype(F32)
                for i in (2 * j, 2 * j + 1)
            ],
            axis=0,
        )
        sig = jax.nn.sigmoid(pre_gate)
        both = jnp.concatenate(
            [
                (hidden * pre_up * sig * (1.0 + pre_gate * (1.0 - sig))).astype(BF),
                (hidden * pre_gate * sig).astype(BF),
            ],
            axis=1,
        )
        ag[pl.ds(x, 1), rows] = both.reshape(1, MC, 2 * HQ)
        for way in range(2):
            start(ag_copy(way, 0, j, x))
        acc[rows] = dot_nt(both, weights(x))

    def ag_stage(k, j):
        rows = pl.ds(j * MC, MC)
        for way in range(2):
            sign = 1 - 2 * way
            src = xat(-sign * k)
            ag_copy(way, k - 1, j, src).wait_recv()
            if k < half_x:
                start(ag_copy(way, k, j, src))
        if k < half_x:
            total = acc[rows]
            for src in (xat(-k), xat(k)):
                block = ag[pl.ds(src, 1), rows].reshape(MC, 2 * HQ)
                total = total + dot_nt(block, weights(src))
            acc[rows] = total
        else:
            src = xat(half_x)
            block = ag[pl.ds(src, 1), rows].reshape(MC, 2 * HQ)
            total = acc[rows] + dot_nt(block, weights(src))
            t_buf[2 * j : 2 * j + 2] = total.astype(BF).reshape(2, NX, CAP2, DQ)
            for i in (2 * j, 2 * j + 1):
                if i:
                    start(y_back(i))

    stages = [functools.partial(rs_stage, k) for k in range(half_x)]
    stages += [act_stage]
    stages += [functools.partial(ag_stage, k) for k in range(1, half_x + 1)]
    for t in range(len(stages) + NCH - 1):
        for j in range(NCH):
            if 0 <= t - j < len(stages):
                stages[t - j](j)

    u_buf[pl.ds(y, 1)] = t_buf[pl.ds(0, 1)]
    for i in range(1, NY):
        ys = yat(-order[i])
        remote(t_buf.at[i], u_buf.at[ys], y2.at[0, i], y2.at[1, i], at_y(ys)).wait_recv()
    for xc in range(NX):
        rows = u_buf[:, xc].reshape(NY * CAP2, DQ)
        sums = dot_tn(sel_buf[xc], rows).astype(BF)
        gp[:, :, xc] = sums.reshape(NZ, CORES, TD, DQ)

    pair = remote(gp.at[:, 1 - c], cx, c2.at[0], c2.at[1], sibling)
    start(pair)
    pair.wait_recv()
    for o in range(1, NZ):
        zd = zat(o)
        mine = gp[pl.ds(zd, 1), pl.ds(c, 1)].reshape(1, NX, TD, DQ).astype(F32)
        q_buf[pl.ds(o, 1)] = (mine + cx[pl.ds(zd, 1)].astype(F32)).astype(BF)
        start(remote(q_buf.at[o], zb.at[o], z2.at[0, o], z2.at[1, o], at_z(zd)))
    total = gp[pl.ds(z, 1), pl.ds(c, 1)].reshape(1, NX, TD, DQ).astype(F32)
    total = total + cx[pl.ds(z, 1)].astype(F32)
    for o in range(1, NZ):
        remote(q_buf.at[o], zb.at[o], z2.at[0, o], z2.at[1, o], at_z(zat(-o))).wait_recv()
        total = total + zb[pl.ds(o, 1)].astype(F32)
    o_buf[...] = total.reshape(NX, TD, DQ).astype(BF)

    for o in range(1, NX):
        xd = xat(o)
        start(remote(o_buf.at[xd], f_buf.at[x], x2.at[0, o], x2.at[1, o], at_x(xd)))
    f_buf[pl.ds(x, 1)] = o_buf[pl.ds(x, 1)]
    for o in range(1, NX):
        xs = xat(-o)
        remote(o_buf.at[xs], f_buf.at[xs], x2.at[0, o], x2.at[1, o], at_x(xs)).wait_recv()
    out[...] = f_buf[...]
    for copy in sends:
        copy.wait_send()


def routes(expert_ids, expert_slot, groups):
    group_of = expert_ids // EXP_GRP
    named = jnp.any(group_of[:, :, None] == jnp.arange(groups)[None, None, :], axis=1)
    rank = jnp.cumsum(named.astype(jnp.int32), axis=0) - 1
    fits = named & (rank < CAP1)
    in_group = jnp.any(
        fits[:, None, :] & (group_of[:, :, None] == jnp.arange(groups)[None, None, :]), axis=2
    )
    admitted = in_group & (expert_slot >= 0)
    names = jnp.where(admitted, expert_ids, 255)
    slots = jnp.where(admitted, expert_slot, 0)
    rest = jnp.zeros((expert_ids.shape[0], META - 16), jnp.int32)
    return jnp.concatenate([names, slots, rest], axis=1).astype(BF)


def shards(tokens, gate_weight, up_weight, hidden_grad, expert_ids, expert_slot):
    NG = lax.axis_size("group")
    NY = EXP_GRP
    NX = lax.axis_size("ingroup") // NY
    NZ = NG // CORES
    TD, D = tokens.shape
    DQ = D // NX
    HQ = hidden_grad.shape[2]
    CAP = hidden_grad.shape[1]
    LANES = DQ + META
    meta = routes(expert_ids, expert_slot, NG)
    blocks = tokens.reshape(TD, NX, DQ).transpose(1, 0, 2)
    blocks = jnp.concatenate([blocks, jnp.broadcast_to(meta[None], (NX, TD, META))], axis=2)
    half_x = NX // 2
    NCH = NY // 2
    vmem = pl.BlockSpec(memory_space=pltpu.VMEM)
    hbm = pl.BlockSpec(memory_space=pl.ANY)
    dma = pltpu.SemaphoreType.DMA
    result = pl.pallas_call(
        functools.partial(kernel, (NX, NY, NZ)),
        out_shape=jax.ShapeDtypeStruct((NX, TD, DQ), BF),
        in_specs=[vmem, hbm, hbm, hbm],
        out_specs=vmem,
        scratch_shapes=[
            pltpu.VMEM((NX, TD, LANES), BF),
            pltpu.VMEM((NX, NG, TD, LANES), BF),
            pltpu.VMEM((NY, NX, CAP2, DQ), BF),
            pltpu.VMEM((NY, NX, CAP2, DQ), BF),
            pltpu.VMEM((NX, DQ, 2 * HQ), BF),
            pltpu.VMEM((CAP, HQ), BF),
            pltpu.VMEM((2, half_x, CAP, 2 * HQ), BF),
            pltpu.VMEM((2, half_x, CAP, 2 * HQ), BF),
            pltpu.VMEM((NX, CAP, 2 * HQ), BF),
            pltpu.VMEM((CAP, DQ), F32),
            pltpu.VMEM((NY, NX, CAP2, DQ), BF),
            pltpu.VMEM((NY, NX, CAP2, DQ), BF),
            pltpu.VMEM((NX, NY * CAP2, NG * TD), BF),
            pltpu.VMEM((NZ, CORES, NX, TD, DQ), BF),
            pltpu.VMEM((NZ, NX, TD, DQ), BF),
            pltpu.VMEM((NZ, NX, TD, DQ), BF),
            pltpu.VMEM((NZ, NX, TD, DQ), BF),
            pltpu.VMEM((NX, TD, DQ), BF),
            pltpu.VMEM((NX, TD, DQ), BF),
            dma((NX * 2,)),
            dma((1,)),
            dma((2, NX)),
            dma((2, NZ)),
            dma((2, NZ)),
            dma((2, NY)),
            dma((2, 2, half_x, NCH)),
            dma((2, 2, half_x, NCH)),
            dma((2, NY)),
            dma((2,)),
            dma((2, NZ)),
            dma((2, NX)),
        ],
        compiler_params=pltpu.CompilerParams(
            collective_id=0, has_side_effects=True, vmem_limit_bytes=VMEM_BYTES
        ),
    )(blocks, gate_weight[0], up_weight[0], hidden_grad[0])
    return result.transpose(1, 0, 2).reshape(TD, D)


def solution(mesh):
    in_specs = (
        P(("group", "ingroup"), None),
        P(("group", "ingroup"), None, None),
        P(("group", "ingroup"), None, None),
        P(("group", "ingroup"), None, None),
        P(("group", "ingroup"), None),
        P(("group", "ingroup"), None),
    )
    out_specs = P(("group", "ingroup"), None)
    return jax.shard_map(shards, mesh=mesh, in_specs=in_specs, out_specs=out_specs, check_vma=False)
```

time: 726 us -> 134 us (0.18)
  waiting for transfers between devices: 500 us -> 0 us
  blocking collectives: 139 us -> 0 us
  Pallas kernels: 0 us -> 126 us
  starting transfers between devices: 67.3 us -> 0 us
    ppermute x12 -> x0, waiting for transfers between devices: 461 us -> none  [partner(): return lax.ppermute(block, axis, route)]
    all_to_all x2 -> x0, blocking collectives: 139 us -> none  [the longest x1 107 us: shards(): lax.all_to_all(group_sums, 'group', split_axis=0, concat_axis=0, tiled=True)]
    pallas_call x0 -> x1, Pallas kernels: none -> 126 us  [shards(): pl.pallas_call(functools.partial(kernel, (NX, NY, NZ)), out_shape=jax.Sha...]
    all_to_all x3 -> x0, waiting for transfers between devices: 38.6 us -> none  [the longest x1 17.5 us: shards(): lax.all_to_all(slot_grad, 'ingroup', split_axis=0, concat_axis=0, tiled=T...]
    ppermute x12 -> x0, starting transfers between devices: 37.7 us -> none  [partner(): return lax.ppermute(block, axis, route)]
    all_to_all x3 -> x0, starting transfers between devices: 29.6 us -> none  [the longest x1 18.2 us: shards(): lax.all_to_all(send_codes, 'group', split_axis=0, concat_axis=0, tiled=True)]
  transfers between devices with their start and end apart: 15 -> 0, of which waited for: 13 -> 0; matrix products, arithmetic and copies ran while one was open for 1% -> 0% of each run, Pallas kernels for 0% -> 0%
where the time goes in v1:
time: 134 us; the launch traced here: 133 us
  Pallas kernels  126 us (94%)
  local copies, waits for them, and re-layouts  4.76 us (4%)
    pallas_call x1, Pallas kernels, shards(): pl.pallas_call(functools.partial(kernel, (NX, NY, NZ)), out_shape=jax.Sha...  126 us
    unnamed x10, local copies, waits for them, and re-layouts  3.75 us

profile of v1, /device:TPU:1, one launch (start us, length us, event | category | flops | bytes accessed | tf_op | source)
XLA Modules:
  0.0 132.6 jit_solution(11022197839402530903)
XLA Ops:
  0.0 0.0 copy-start.4
  0.0 0.0 copy-start.3
  0.0 0.1 pad.4.clone
  0.1 0.6 copy-done.4
  0.7 0.1 fusion.1
  0.8 0.3 fusion.2
  1.1 0.7 select_convert_fusion.1
  1.8 0.1 maximum_maximum_fusion
  1.9 0.0 copy-done.3
  1.9 0.1 reshape.39
  2.1 0.0 copy-start.2
  2.1 0.1 pad_maximum_fusion.tok
  2.2 0.8 copy-done.2
  3.0 0.0 copy-start
  3.0 1.2 copy-done
  4.1 0.0 copy-start.1
  4.2 1.2 copy-done.1
  5.3 126.4 %shard_map.64 = bf16[8,8,448]{2,1,0:T(8,128)(2,1)S(1)} custom-call(bf16[8,8,512]{2,1,0:T(8,128)(2,1)S(1)} %pad_maximum_fusion.tok, bf16[448,1024]{1,0:T(8,128)(2,1)S(1)} %bitcast.7, bf16[448,1024]{1,0:T(8,128)(2,1)S(1)} %bitcast.8, bf16[512,128]{1,0:T(8,128)(2,1)S(1)} %bitcast.10), custom_call_target="tpu_custom_call" | custom-call | tf_op jit(solution)/shard_map/pallas_call | solution.py:385
  131.8 0.7 reshape.40
  (8 shorter events, 0.1 us)
Async XLA Ops:
  0.0 0.7 copy-start.4
  0.0 1.9 %copy-start.3 = (bf16[8,3584]{1,0:T(8,128)(2,1)S(1)}, bf16[8,3584]{1,0:T(8,128)(2,1)}, u32[]{:S(2)}) copy-start(bf16[8,3584]{1,0:T(8,128)(2,1)} %param.6) | copy-start | bytes 172036
  2.1 0.9 copy-start.2
  3.0 1.2 copy-start
  4.1 1.2 copy-start.1

commit v2 on v1

v2 whole, which is shorter than its diff:
```python
import functools

import jax
import jax.numpy as jnp
from jax import lax
from jax.experimental import pallas as pl
from jax.experimental.pallas import tpu as pltpu
from jax.sharding import PartitionSpec as P

MESH = pl.DeviceIdType.MESH
BF = jnp.bfloat16
F32 = jnp.float32
CORES = 2
EXP_GRP = 8
CAP1 = 4
CAP2 = 8
META = 64
CPC = 2
VMEM_BYTES = 48 * 1024 * 1024


def remote(src, dst, send_sem, recv_sem, device):
    return pltpu.make_async_remote_copy(
        src_ref=src,
        dst_ref=dst,
        send_sem=send_sem,
        recv_sem=recv_sem,
        device_id=device,
        device_id_type=MESH,
    )


def dot_nt(a, b):
    return lax.dot_general(a, b, (((1,), (1,)), ((), ())), preferred_element_type=F32)


def dot_tn(a, b):
    return lax.dot_general(a, b, (((0,), (0,)), ((), ())), preferred_element_type=F32)


def kernel(
    dims,
    tokens,
    ids,
    slots,
    wg,
    wu,
    hg,
    out,
    tok_in,
    ids_in,
    slots_in,
    tok,
    a_buf,
    g_buf,
    s_buf,
    r_buf,
    w2,
    h_buf,
    rs_s,
    rs_r,
    ag,
    acc,
    t_buf,
    u_buf,
    sel_buf,
    gp,
    cx,
    q_buf,
    zb,
    o_buf,
    f_buf,
    in_sem,
    w_sem,
    x1,
    z1,
    c1,
    y1,
    rs_sem,
    ag_sem,
    y2,
    c2,
    z2,
    x2,
):
    NX, NY, NZ = dims
    NG = NZ * CORES
    TD = tok.shape[1]
    LANES = tok.shape[2]
    DQ = LANES - META
    HQ = hg.shape[1]
    RG = NX * CAP2
    CR = CPC * CAP2
    MC = NY * CR
    HALF = MC // 2
    NCH = NX // CPC
    half_x = NX // 2

    g = lax.axis_index("group")
    p = lax.axis_index("ingroup")
    z, c = lax.div(g, CORES), lax.rem(g, CORES)
    y, x = lax.div(p, NX), lax.rem(p, NX)

    def xat(o):
        return lax.rem(x + (o + NX), NX)

    def yat(o):
        return lax.rem(y + (o + NY), NY)

    def zat(o):
        return lax.rem(z + (o + NZ), NZ)

    def at_x(xx):
        return (g, y * NX + xx)

    def at_y(yy):
        return (g, yy * NX + x)

    def at_z(zz):
        return (zz * CORES + c, p)

    sibling = (z * CORES + (1 - c), p)
    sends = []

    def start(copy):
        copy.start()
        sends.append(copy)

    inputs = [
        pltpu.make_async_copy(ids, ids_in, in_sem.at[0]),
        pltpu.make_async_copy(slots, slots_in, in_sem.at[1]),
        pltpu.make_async_copy(tokens, tok_in, in_sem.at[2]),
    ]
    for load in inputs:
        load.start()

    barrier = pltpu.get_barrier_semaphore()
    peers = [at_x(xat(o)) for o in range(1, NX)]
    peers += [at_y(yat(o)) for o in range(1, NY)]
    peers += [at_z(zat(o)) for o in range(1, NZ)]
    peers += [sibling]
    for peer in peers:
        pl.semaphore_signal(barrier, inc=1, device_id=peer, device_id_type=MESH)

    loads = []
    for d in range(NX):
        for n, w in enumerate((wg, wu)):
            loads.append(
                pltpu.make_async_copy(
                    w.at[:, pl.ds(d * HQ, HQ)],
                    w2.at[d, :, pl.ds(n * HQ, HQ)],
                    w_sem.at[d * 2 + n],
                )
            )
    loads.append(pltpu.make_async_copy(hg, h_buf, in_sem.at[3]))
    for load in loads:
        load.start()
    for load in inputs:
        load.wait()

    names, places = ids_in[...], slots_in[...]
    group_of = lax.div(names, EXP_GRP)
    lane = lax.broadcasted_iota(jnp.int32, (TD, 128), 1)
    named = jnp.zeros((TD, 128), F32)
    for k in range(names.shape[1]):
        named = jnp.where(group_of[:, k : k + 1] == lane, 1.0, named)
    before = lax.broadcasted_iota(jnp.int32, (TD, TD), 1) < lax.broadcasted_iota(jnp.int32, (TD, TD), 0)
    rank = jnp.dot(
        jnp.where(before, 1.0, 0.0).astype(BF), named.astype(BF), preferred_element_type=F32
    )
    fits = jnp.where(rank < CAP1, named, 0.0)
    meta = jnp.zeros((TD, 128), F32)
    for k in range(names.shape[1]):
        in_group = jnp.sum(jnp.where(group_of[:, k : k + 1] == lane, fits, 0.0), axis=1, keepdims=True)
        place = places[:, k : k + 1]
        name = jnp.where((in_group > 0.0) & (place >= 0), names[:, k : k + 1], 255).astype(F32)
        meta = jnp.where(lane == k, name, meta)
        meta = jnp.where(lane == 8 + k, jnp.maximum(place, 0).astype(F32), meta)
    features = tok_in[...].astype(F32)
    for d in range(NX):
        block = jnp.concatenate([features[:, d * DQ : (d + 1) * DQ], meta[:, :META]], axis=1)
        tok[d] = block.astype(BF)
    pl.semaphore_wait(barrier, len(peers))

    for o in range(1, NX):
        xd = xat(o)
        start(remote(tok.at[xd], a_buf.at[x], x1.at[0, o], x1.at[1, o], at_x(xd)))
    a_buf[pl.ds(x, 1)] = tok[pl.ds(x, 1)]
    for o in range(1, NX):
        xs = xat(-o)
        remote(tok.at[xs], a_buf.at[xs], x1.at[0, o], x1.at[1, o], at_x(xs)).wait_recv()

    def z_copy(o, j, src, dst):
        cols = pl.ds(j * CPC, CPC)
        return remote(
            a_buf.at[cols], g_buf.at[cols, src, c], z1.at[0, o, j], z1.at[1, o, j], at_z(dst)
        )

    for j in range(NCH):
        for o in range(1, NZ):
            start(z_copy(o, j, z, zat(o)))
    g_buf[:, pl.ds(z, 1), pl.ds(c, 1)] = a_buf[...].reshape(NX, 1, 1, TD, LANES)

    def core_copy(j, core):
        part = g_buf.at[pl.ds(j * CPC, CPC), :, core]
        return remote(part, part, c1.at[0, j], c1.at[1, j], sibling)

    def gather_stage(j):
        for o in range(1, NZ):
            z_copy(o, j, zat(-o), zat(-o)).wait_recv()
        start(core_copy(j, c))

    pick_row = lax.broadcasted_iota(jnp.int32, (8, 128), 0)
    pick_lane = lax.broadcasted_iota(jnp.int32, (8, 128), 1) - (128 - META)
    pick = jnp.where(pick_lane == pick_row, 8.0, jnp.where(pick_lane == 8 + pick_row, 1.0, 0.0))
    pick = pick.astype(BF)
    code_of = lax.broadcasted_iota(jnp.int32, (NY * CAP2, NG * TD), 0) + g * (NY * CAP2)
    code_of = code_of.astype(F32)

    def y_copy(o, j, src, dst):
        return remote(
            s_buf.at[j, dst], r_buf.at[j, src], y1.at[0, o, j], y1.at[1, o, j], at_y(dst)
        )

    def pick_stage(j):
        core_copy(j, 1 - c).wait_recv()
        for q in range(CPC):
            xc = j * CPC + q
            rows = g_buf[xc].reshape(NG * TD, LANES)
            codes = dot_nt(pick, rows[:, LANES - 128 :])
            sel = jnp.zeros(code_of.shape, F32)
            for k in range(8):
                sel = jnp.where(codes[k : k + 1, :] == code_of, 1.0, sel)
            sel = sel.astype(BF)
            sel_buf[xc] = sel
            picked = jnp.dot(sel, rows[:, :DQ], preferred_element_type=F32).astype(BF)
            s_buf[j, :, q] = picked.reshape(NY, CAP2, DQ)
        for o in range(1, NY):
            start(y_copy(o, j, y, yat(o)))
        r_buf[j, pl.ds(y, 1)] = s_buf[j, pl.ds(y, 1)]

    def weights(d):
        return w2[pl.ds(d, 1)].reshape(DQ, 2 * HQ)

    def slot_rows(j):
        return r_buf[j].reshape(MC, DQ)

    def rs_copy(way, k, j):
        rows = pl.ds(j * MC, MC) if k else pl.ds(j * MC + way * HALF, HALF)
        return remote(
            rs_s.at[way, k, rows],
            rs_r.at[way, k, rows],
            rs_sem.at[0, way, k, j],
            rs_sem.at[1, way, k, j],
            at_x(xat(1 - 2 * way)),
        )

    def ag_copy(way, k, j, src):
        rows = pl.ds(j * MC, MC) if k < half_x - 1 else pl.ds(j * MC + way * HALF, HALF)
        return remote(
            ag.at[src, rows],
            ag.at[src, rows],
            ag_sem.at[0, way, k, j],
            ag_sem.at[1, way, k, j],
            at_x(xat(1 - 2 * way)),
        )

    def rs_stage(k, j):
        if k == 0:
            for o in range(1, NY):
                y_copy(o, j, yat(-o), yat(-o)).wait_recv()
            if j == 0:
                for load in loads:
                    load.wait()
        base = j * MC
        lhs = slot_rows(j)
        for way in range(2):
            sign = 1 - 2 * way
            w = weights(xat(sign * (half_x - k)))
            mine = pl.ds(base + way * HALF, HALF)
            other = pl.ds(base + (1 - way) * HALF, HALF)
            if k == 0:
                part = lhs[way * HALF : way * HALF + HALF]
                rs_s[way, 0, mine] = jnp.dot(part, w, preferred_element_type=F32).astype(BF)
            else:
                part = jnp.dot(lhs, w, preferred_element_type=F32)
                rs_copy(way, k - 1, j).wait_recv()
                if k == 1:
                    own = part[way * HALF : way * HALF + HALF]
                    rest = part[(1 - way) * HALF : (1 - way) * HALF + HALF]
                    rs_s[way, 1, mine] = (own + rs_r[way, 0, mine].astype(F32)).astype(BF)
                    rs_s[way, 1, other] = rest.astype(BF)
                else:
                    rows = pl.ds(base, MC)
                    rs_s[way, k, rows] = (part + rs_r[way, k - 1, rows].astype(F32)).astype(BF)
            start(rs_copy(way, k, j))

    def act_stage(j):
        rows = pl.ds(j * MC, MC)
        pre = jnp.dot(slot_rows(j), weights(x), preferred_element_type=F32)
        for way in range(2):
            rs_copy(way, half_x - 1, j).wait_recv()
            pre = pre + rs_r[way, half_x - 1, rows].astype(F32)
        pre_gate, pre_up = pre[:, :HQ], pre[:, HQ:]
        hidden = jnp.concatenate(
            [h_buf[ys * RG + j * CR : ys * RG + (j + 1) * CR] for ys in range(NY)], axis=0
        ).astype(F32)
        sig = jax.nn.sigmoid(pre_gate)
        both = jnp.concatenate(
            [
                (hidden * pre_up * sig * (1.0 + pre_gate * (1.0 - sig))).astype(BF),
                (hidden * pre_gate * sig).astype(BF),
            ],
            axis=1,
        )
        ag[pl.ds(x, 1), rows] = both.reshape(1, MC, 2 * HQ)
        for way in range(2):
            start(ag_copy(way, 0, j, x))
        acc[rows] = dot_nt(both, weights(x))

    def back_copy(o, j, src, dst):
        return remote(
            t_buf.at[j, dst], u_buf.at[j, src], y2.at[0, o, j], y2.at[1, o, j], at_y(dst)
        )

    def ag_stage(k, j):
        rows = pl.ds(j * MC, MC)
        for way in range(2):
            sign = 1 - 2 * way
            src = xat(-sign * k)
            ag_copy(way, k - 1, j, src).wait_recv()
            if k < half_x:
                start(ag_copy(way, k, j, src))
        if k < half_x:
            total = acc[rows]
            for src in (xat(-k), xat(k)):
                block = ag[pl.ds(src, 1), rows].reshape(MC, 2 * HQ)
                total = total + dot_nt(block, weights(src))
            acc[rows] = total
        else:
            src = xat(half_x)
            block = ag[pl.ds(src, 1), rows].reshape(MC, 2 * HQ)
            total = acc[rows] + dot_nt(block, weights(src))
            t_buf[j] = total.astype(BF).reshape(NY, CPC, CAP2, DQ)
            for o in range(1, NY):
                start(back_copy(o, j, y, yat(o)))
            u_buf[j, pl.ds(y, 1)] = t_buf[j, pl.ds(y, 1)]

    def pair_copy(j):
        return remote(gp.at[j, :, 1 - c], cx.at[j], c2.at[0, j], c2.at[1, j], sibling)

    def group_stage(j):
        for o in range(1, NY):
            back_copy(o, j, yat(-o), yat(-o)).wait_recv()
        for q in range(CPC):
            rows = u_buf[j, :, q].reshape(NY * CAP2, DQ)
            sums = dot_tn(sel_buf[j * CPC + q], rows).astype(BF)
            gp[j, :, :, q] = sums.reshape(NZ, CORES, TD, DQ)
        start(pair_copy(j))

    def sum_copy(o, j, dst):
        return remote(q_buf.at[j, o], zb.at[j, o], z2.at[0, o, j], z2.at[1, o, j], at_z(dst))

    def pair_sum(j, zd):
        mine = gp[j, pl.ds(zd, 1), pl.ds(c, 1)].reshape(CPC, TD, DQ).astype(F32)
        return mine + cx[j, pl.ds(zd, 1)].reshape(CPC, TD, DQ).astype(F32)

    def pair_stage(j):
        pair_copy(j).wait_recv()
        for o in range(1, NZ):
            zd = zat(o)
            q_buf[j, o] = pair_sum(j, zd).astype(BF)
            start(sum_copy(o, j, zd))

    def sum_stage(j):
        total = pair_sum(j, z)
        for o in range(1, NZ):
            sum_copy(o, j, zat(-o)).wait_recv()
            total = total + zb[j, o].astype(F32)
        o_buf[j * CPC : (j + 1) * CPC] = total.astype(BF)

    stages = [gather_stage, pick_stage]
    stages += [functools.partial(rs_stage, k) for k in range(half_x)]
    stages += [act_stage]
    stages += [functools.partial(ag_stage, k) for k in range(1, half_x + 1)]
    stages += [group_stage, pair_stage, sum_stage]
    for t in range(len(stages) + NCH - 1):
        for j in range(NCH):
            if 0 <= t - j < len(stages):
                stages[t - j](j)

    for o in range(1, NX):
        xd = xat(o)
        start(remote(o_buf.at[xd], f_buf.at[x], x2.at[0, o], x2.at[1, o], at_x(xd)))
    f_buf[pl.ds(x, 1)] = o_buf[pl.ds(x, 1)]
    for o in range(1, NX):
        xs = xat(-o)
        remote(o_buf.at[xs], f_buf.at[xs], x2.at[0, o], x2.at[1, o], at_x(xs)).wait_recv()
    out[...] = jnp.concatenate([f_buf[d].astype(F32) for d in range(NX)], axis=1).astype(BF)
    for copy in sends:
        copy.wait_send()


def shards(tokens, gate_weight, up_weight, hidden_grad, expert_ids, expert_slot):
    NG = lax.axis_size("group")
    NY = EXP_GRP
    NX = lax.axis_size("ingroup") // NY
    NZ = NG // CORES
    TD, D = tokens.shape
    DQ = D // NX
    HQ = hidden_grad.shape[2]
    CAP = hidden_grad.shape[1]
    LANES = DQ + META
    half_x = NX // 2
    NCH = NX // CPC
    hbm = pl.BlockSpec(memory_space=pltpu.HBM)
    dma = pltpu.SemaphoreType.DMA
    return pl.pallas_call(
        functools.partial(kernel, (NX, NY, NZ)),
        out_shape=jax.ShapeDtypeStruct((TD, D), BF),
        in_specs=[hbm] * 6,
        out_specs=pl.BlockSpec(memory_space=pltpu.VMEM),
        scratch_shapes=[
            pltpu.VMEM(tokens.shape, BF),
            pltpu.VMEM(expert_ids.shape, jnp.int32),
            pltpu.VMEM(expert_slot.shape, jnp.int32),
            pltpu.VMEM((NX, TD, LANES), BF),
            pltpu.VMEM((NX, TD, LANES), BF),
            pltpu.VMEM((NX, NZ, CORES, TD, LANES), BF),
            pltpu.VMEM((NCH, NY, CPC, CAP2, DQ), BF),
            pltpu.VMEM((NCH, NY, CPC, CAP2, DQ), BF),
            pltpu.VMEM((NX, DQ, 2 * HQ), BF),
            pltpu.VMEM((CAP, HQ), BF),
            pltpu.VMEM((2, half_x, CAP, 2 * HQ), BF),
            pltpu.VMEM((2, half_x, CAP, 2 * HQ), BF),
            pltpu.VMEM((NX, CAP, 2 * HQ), BF),
            pltpu.VMEM((CAP, DQ), F32),
            pltpu.VMEM((NCH, NY, CPC, CAP2, DQ), BF),
            pltpu.VMEM((NCH, NY, CPC, CAP2, DQ), BF),
            pltpu.VMEM((NX, NY * CAP2, NG * TD), BF),
            pltpu.VMEM((NCH, NZ, CORES, CPC, TD, DQ), BF),
            pltpu.VMEM((NCH, NZ, CPC, TD, DQ), BF),
            pltpu.VMEM((NCH, NZ, CPC, TD, DQ), BF),
            pltpu.VMEM((NCH, NZ, CPC, TD, DQ), BF),
            pltpu.VMEM((NX, TD, DQ), BF),
            pltpu.VMEM((NX, TD, DQ), BF),
            dma((4,)),
            dma((NX * 2,)),
            dma((2, NX)),
            dma((2, NZ, NCH)),
            dma((2, NCH)),
            dma((2, NY, NCH)),
            dma((2, 2, half_x, NCH)),
            dma((2, 2, half_x, NCH)),
            dma((2, NY, NCH)),
            dma((2, NCH)),
            dma((2, NZ, NCH)),
            dma((2, NX)),
        ],
        compiler_params=pltpu.CompilerParams(
            collective_id=0, has_side_effects=True, vmem_limit_bytes=VMEM_BYTES
        ),
    )(tokens, expert_ids, expert_slot, gate_weight[0], up_weight[0], hidden_grad[0])


def solution(mesh):
    in_specs = (
        P(("group", "ingroup"), None),
        P(("group", "ingroup"), None, None),
        P(("group", "ingroup"), None, None),
        P(("group", "ingroup"), None, None),
        P(("group", "ingroup"), None),
        P(("group", "ingroup"), None),
    )
    out_specs = P(("group", "ingroup"), None)
    return jax.shard_map(shards, mesh=mesh, in_specs=in_specs, out_specs=out_specs, check_vma=False)
```

time: 134 us -> 132 us (0.985)
    unnamed x10 -> x13, local copies, waits for them, and re-layouts: 3.75 us -> 6.08 us
    pallas_call x1, Pallas kernels: 126 us -> 125 us  [shards(): pl.pallas_call(functools.partial(kernel, (NX, NY, NZ)), out_shape=jax.Sha...]
where the time goes in v2:
time: 132 us; the launch traced here: 131 us
  Pallas kernels  125 us (95%)
  local copies, waits for them, and re-layouts  6.08 us (5%)
    pallas_call x1, Pallas kernels, shards(): pl.pallas_call(functools.partial(kernel, (NX, NY, NZ)), out_shape=jax.Sha...  125 us
    unnamed x13, local copies, waits for them, and re-layouts  6.08 us

profile of v2, /device:TPU:1, one launch (start us, length us, event | category | flops | bytes accessed | tf_op | source)
XLA Modules:
  0.0 131.1 jit_solution(10999745965736549335)
XLA Ops:
  0.0 0.0 copy-start.4
  0.0 0.7 copy-done.4
  0.7 0.0 copy-start
  0.7 1.2 copy-done
  1.9 0.0 copy-start.1
  1.9 1.2 copy-done.1
  3.0 0.0 copy-start.2
  3.0 0.9 copy-done.2
  4.0 0.0 copy-start.3
  4.0 0.8 copy-done.3
  4.8 0.0 copy-start.5
  4.8 0.7 copy-done.5
  5.5 125.1 %shard_map.64 = bf16[8,3584]{1,0:T(8,128)(2,1)S(1)} custom-call(bf16[8,3584]{1,0:T(8,128)(2,1)S(1)} %copy-done.3, s32[8,8]{1,0:T(8,128)S(1)} %copy-done.4, s32[8,8]{1,0:T(8,128)S(1)} %copy-done.5, bf16[448,1024]{1,0:T(8,128)(2,1)S(1)} %bitcast.3, bf16[448,1024]{1,0:T(8,128)(2,1)S(1)} %bitcast.4, bf16[512,128]{1,0:T(8,128)(2,1)S(1)} %bitcast.5), custom_call_target="tpu_custom_call" | custom-call | tf_op jit(solution)/shard_map/pallas_call | solution.py:418
  130.5 0.6 copy.8
Async XLA Ops:
  0.0 0.7 copy-start.4
  0.7 1.2 copy-start
  1.9 1.2 copy-start.1
  3.0 0.9 copy-start.2
  4.0 0.8 copy-start.3
  4.8 0.7 copy-start.5

commit v3 on v2

--- a/solution.py
+++ b/solution.py
@@ -15,8 +15,12 @@
 CAP1 = 4
 CAP2 = 8
 META = 64
-CPC = 2
-VMEM_BYTES = 48 * 1024 * 1024
+CHUNKS = (2, 2, 2, 2)
+ORDER = (
+    0, 0, 1, 0, 1, 0, 2, 0, 1, 2, 1, 0, 3, 2, 3, 1, 0, 2, 1, 3, 0, 2, 3, 1, 0, 2, 3, 1, 0, 2, 3,
+    0, 1, 2, 3, 0, 1, 2, 0, 3, 1, 2, 3, 2, 0, 1, 3, 1, 3, 2, 2, 1, 3, 3, 2, 3,
+)
+VMEM_BYTES = 62 * 1024 * 1024
 
 
 def remote(src, dst, send_sem, recv_sem, device):
@@ -90,10 +94,10 @@
     DQ = LANES - META
     HQ = hg.shape[1]
     RG = NX * CAP2
-    CR = CPC * CAP2
-    MC = NY * CR
-    HALF = MC // 2
-    NCH = NX // CPC
+    CHUNK_ROWS = NY * CAP2
+    NCH = len(CHUNKS)
+    first = [sum(CHUNKS[:j]) for j in range(NCH)]
+    assert sum(CHUNKS) == NX
     half_x = NX // 2
 
     g = lax.axis_index("group")
@@ -191,24 +195,28 @@
         remote(tok.at[xs], a_buf.at[xs], x1.at[0, o], x1.at[1, o], at_x(xs)).wait_recv()
 
     def z_copy(o, j, src, dst):
-        cols = pl.ds(j * CPC, CPC)
+        cols = pl.ds(first[j], CHUNKS[j])
         return remote(
             a_buf.at[cols], g_buf.at[cols, src, c], z1.at[0, o, j], z1.at[1, o, j], at_z(dst)
         )
 
-    for j in range(NCH):
+    def z_send(j):
         for o in range(1, NZ):
             start(z_copy(o, j, z, zat(o)))
+
+    z_send(0)
     g_buf[:, pl.ds(z, 1), pl.ds(c, 1)] = a_buf[...].reshape(NX, 1, 1, TD, LANES)
 
     def core_copy(j, core):
-        part = g_buf.at[pl.ds(j * CPC, CPC), :, core]
+        part = g_buf.at[pl.ds(first[j], CHUNKS[j]), :, core]
         return remote(part, part, c1.at[0, j], c1.at[1, j], sibling)
 
     def gather_stage(j):
         for o in range(1, NZ):
             z_copy(o, j, zat(-o), zat(-o)).wait_recv()
         start(core_copy(j, c))
+        if j + 1 < NCH:
+            z_send(j + 1)
 
     pick_row = lax.broadcasted_iota(jnp.int32, (8, 128), 0)
     pick_lane = lax.broadcasted_iota(jnp.int32, (8, 128), 1) - (128 - META)
@@ -217,15 +225,18 @@
     code_of = lax.broadcasted_iota(jnp.int32, (NY * CAP2, NG * TD), 0) + g * (NY * CAP2)
     code_of = code_of.astype(F32)
 
+    def blocks(j, row):
+        return pl.ds(first[j] * NY + row * CHUNKS[j], CHUNKS[j])
+
     def y_copy(o, j, src, dst):
         return remote(
-            s_buf.at[j, dst], r_buf.at[j, src], y1.at[0, o, j], y1.at[1, o, j], at_y(dst)
+            s_buf.at[blocks(j, dst)], r_buf.at[blocks(j, src)], y1.at[0, o, j], y1.at[1, o, j], at_y(dst)
         )
 
     def pick_stage(j):
         core_copy(j, 1 - c).wait_recv()
-        for q in range(CPC):
-            xc = j * CPC + q
+        for q in range(CHUNKS[j]):
+            xc = first[j] + q
             rows = g_buf[xc].reshape(NG * TD, LANES)
             codes = dot_nt(pick, rows[:, LANES - 128 :])
             sel = jnp.zeros(code_of.shape, F32)
@@ -234,19 +245,26 @@
             sel = sel.astype(BF)
             sel_buf[xc] = sel
             picked = jnp.dot(sel, rows[:, :DQ], preferred_element_type=F32).astype(BF)
-            s_buf[j, :, q] = picked.reshape(NY, CAP2, DQ)
+            for e in range(NY):
+                s_buf[first[j] * NY + e * CHUNKS[j] + q] = picked[e * CAP2 : (e + 1) * CAP2]
         for o in range(1, NY):
             start(y_copy(o, j, y, yat(o)))
-        r_buf[j, pl.ds(y, 1)] = s_buf[j, pl.ds(y, 1)]
+        r_buf[blocks(j, y)] = s_buf[blocks(j, y)]
 
     def weights(d):
         return w2[pl.ds(d, 1)].reshape(DQ, 2 * HQ)
 
+    def span(j, half=None):
+        base, size = first[j] * CHUNK_ROWS, CHUNKS[j] * CHUNK_ROWS
+        if half is None:
+            return pl.ds(base, size)
+        return pl.ds(base + half * (size // 2), size // 2)
+
     def slot_rows(j):
-        return r_buf[j].reshape(MC, DQ)
+        return r_buf[first[j] * NY : (first[j] + CHUNKS[j]) * NY].reshape(CHUNKS[j] * CHUNK_ROWS, DQ)
 
     def rs_copy(way, k, j):
-        rows = pl.ds(j * MC, MC) if k else pl.ds(j * MC + way * HALF, HALF)
+        rows = span(j, None if k else way)
         return remote(
             rs_s.at[way, k, rows],
             rs_r.at[way, k, rows],
@@ -256,7 +274,7 @@
         )
 
     def ag_copy(way, k, j, src):
-        rows = pl.ds(j * MC, MC) if k < half_x - 1 else pl.ds(j * MC + way * HALF, HALF)
+        rows = span(j, None if k < half_x - 1 else way)
         return remote(
             ag.at[src, rows],
             ag.at[src, rows],
@@ -272,38 +290,42 @@
             if j == 0:
                 for load in loads:
                     load.wait()
-        base = j * MC
+        size = CHUNKS[j] * CHUNK_ROWS // 2
         lhs = slot_rows(j)
         for way in range(2):
             sign = 1 - 2 * way
             w = weights(xat(sign * (half_x - k)))
-            mine = pl.ds(base + way * HALF, HALF)
-            other = pl.ds(base + (1 - way) * HALF, HALF)
+            mine = span(j, way)
+            other = span(j, 1 - way)
             if k == 0:
-                part = lhs[way * HALF : way * HALF + HALF]
+                part = lhs[way * size : way * size + size]
                 rs_s[way, 0, mine] = jnp.dot(part, w, preferred_element_type=F32).astype(BF)
             else:
                 part = jnp.dot(lhs, w, preferred_element_type=F32)
                 rs_copy(way, k - 1, j).wait_recv()
                 if k == 1:
-                    own = part[way * HALF : way * HALF + HALF]
-                    rest = part[(1 - way) * HALF : (1 - way) * HALF + HALF]
+                    own = part[way * size : way * size + size]
+                    rest = part[(1 - way) * size : (1 - way) * size + size]
                     rs_s[way, 1, mine] = (own + rs_r[way, 0, mine].astype(F32)).astype(BF)
                     rs_s[way, 1, other] = rest.astype(BF)
                 else:
-                    rows = pl.ds(base, MC)
+                    rows = span(j)
                     rs_s[way, k, rows] = (part + rs_r[way, k - 1, rows].astype(F32)).astype(BF)
             start(rs_copy(way, k, j))
 
     def act_stage(j):
-        rows = pl.ds(j * MC, MC)
+        rows = span(j)
         pre = jnp.dot(slot_rows(j), weights(x), preferred_element_type=F32)
         for way in range(2):
             rs_copy(way, half_x - 1, j).wait_recv()
             pre = pre + rs_r[way, half_x - 1, rows].astype(F32)
         pre_gate, pre_up = pre[:, :HQ], pre[:, HQ:]
         hidden = jnp.concatenate(
-            [h_buf[ys * RG + j * CR : ys * RG + (j + 1) * CR] for ys in range(NY)], axis=0
+            [
+                h_buf[ys * RG + first[j] * CAP2 : ys * RG + (first[j] + CHUNKS[j]) * CAP2]
+                for ys in range(NY)
+            ],
+            axis=0,
         ).astype(F32)
         sig = jax.nn.sigmoid(pre_gate)
         both = jnp.concatenate(
@@ -313,18 +335,18 @@
             ],
             axis=1,
         )
-        ag[pl.ds(x, 1), rows] = both.reshape(1, MC, 2 * HQ)
+        ag[pl.ds(x, 1), rows] = both.reshape(1, CHUNKS[j] * CHUNK_ROWS, 2 * HQ)
         for way in range(2):
             start(ag_copy(way, 0, j, x))
         acc[rows] = dot_nt(both, weights(x))
 
     def back_copy(o, j, src, dst):
         return remote(
-            t_buf.at[j, dst], u_buf.at[j, src], y2.at[0, o, j], y2.at[1, o, j], at_y(dst)
+            t_buf.at[blocks(j, dst)], u_buf.at[blocks(j, src)], y2.at[0, o, j], y2.at[1, o, j], at_y(dst)
         )
 
     def ag_stage(k, j):
-        rows = pl.ds(j * MC, MC)
+        rows = span(j)
         for way in range(2):
             sign = 1 - 2 * way
             src = xat(-sign * k)
@@ -334,60 +356,66 @@
         if k < half_x:
             total = acc[rows]
             for src in (xat(-k), xat(k)):
-                block = ag[pl.ds(src, 1), rows].reshape(MC, 2 * HQ)
+                block = ag[pl.ds(src, 1), rows].reshape(CHUNKS[j] * CHUNK_ROWS, 2 * HQ)
                 total = total + dot_nt(block, weights(src))
             acc[rows] = total
         else:
             src = xat(half_x)
-            block = ag[pl.ds(src, 1), rows].reshape(MC, 2 * HQ)
+            block = ag[pl.ds(src, 1), rows].reshape(CHUNKS[j] * CHUNK_ROWS, 2 * HQ)
             total = acc[rows] + dot_nt(block, weights(src))
-            t_buf[j] = total.astype(BF).reshape(NY, CPC, CAP2, DQ)
+            t_buf[first[j] * NY : (first[j] + CHUNKS[j]) * NY] = total.astype(BF).reshape(-1, CAP2, DQ)
             for o in range(1, NY):
                 start(back_copy(o, j, y, yat(o)))
-            u_buf[j, pl.ds(y, 1)] = t_buf[j, pl.ds(y, 1)]
+            u_buf[blocks(j, y)] = t_buf[blocks(j, y)]
 
     def pair_copy(j):
-        return remote(gp.at[j, :, 1 - c], cx.at[j], c2.at[0, j], c2.at[1, j], sibling)
+        away = pl.ds((first[j] * CORES + (1 - c) * CHUNKS[j]) * NZ, CHUNKS[j] * NZ)
+        return remote(gp.at[away], cx.at[pl.ds(first[j] * NZ, CHUNKS[j] * NZ)], c2.at[0, j], c2.at[1, j], sibling)
 
     def group_stage(j):
         for o in range(1, NY):
             back_copy(o, j, yat(-o), yat(-o)).wait_recv()
-        for q in range(CPC):
-            rows = u_buf[j, :, q].reshape(NY * CAP2, DQ)
-            sums = dot_tn(sel_buf[j * CPC + q], rows).astype(BF)
-            gp[j, :, :, q] = sums.reshape(NZ, CORES, TD, DQ)
+        n = CHUNKS[j]
+        for q in range(n):
+            rows = jnp.concatenate([u_buf[first[j] * NY + e * n + q] for e in range(NY)], axis=0)
+            sums = dot_tn(sel_buf[first[j] + q], rows).astype(BF)
+            for zz in range(NZ):
+                for cc in range(CORES):
+                    row = (zz * CORES + cc) * TD
+                    gp[(first[j] * CORES + cc * n) * NZ + zz * n + q] = sums[row : row + TD]
         start(pair_copy(j))
 
     def sum_copy(o, j, dst):
-        return remote(q_buf.at[j, o], zb.at[j, o], z2.at[0, o, j], z2.at[1, o, j], at_z(dst))
+        part = pl.ds(first[j] * NZ + o * CHUNKS[j], CHUNKS[j])
+        return remote(q_buf.at[part], zb.at[part], z2.at[0, o, j], z2.at[1, o, j], at_z(dst))
 
     def pair_sum(j, zd):
-        mine = gp[j, pl.ds(zd, 1), pl.ds(c, 1)].reshape(CPC, TD, DQ).astype(F32)
-        return mine + cx[j, pl.ds(zd, 1)].reshape(CPC, TD, DQ).astype(F32)
+        n = CHUNKS[j]
+        mine = gp[pl.ds((first[j] * CORES + c * n) * NZ + zd * n, n)].astype(F32)
+        return mine + cx[pl.ds(first[j] * NZ + zd * n, n)].astype(F32)
 
     def pair_stage(j):
         pair_copy(j).wait_recv()
         for o in range(1, NZ):
             zd = zat(o)
-            q_buf[j, o] = pair_sum(j, zd).astype(BF)
+            q_buf[first[j] * NZ + o * CHUNKS[j] : first[j] * NZ + (o + 1) * CHUNKS[j]] = pair_sum(j, zd).astype(BF)
             start(sum_copy(o, j, zd))
 
     def sum_stage(j):
         total = pair_sum(j, z)
         for o in range(1, NZ):
             sum_copy(o, j, zat(-o)).wait_recv()
-            total = total + zb[j, o].astype(F32)
-        o_buf[j * CPC : (j + 1) * CPC] = total.astype(BF)
+            total = total + zb[first[j] * NZ + o * CHUNKS[j] : first[j] * NZ + (o + 1) * CHUNKS[j]].astype(F32)
+        o_buf[first[j] : first[j] + CHUNKS[j]] = total.astype(BF)
 
     stages = [gather_stage, pick_stage]
     stages += [functools.partial(rs_stage, k) for k in range(half_x)]
     stages += [act_stage]
     stages += [functools.partial(ag_stage, k) for k in range(1, half_x + 1)]
     stages += [group_stage, pair_stage, sum_stage]
-    for t in range(len(stages) + NCH - 1):
-        for j in range(NCH):
-            if 0 <= t - j < len(stages):
-                stages[t - j](j)
+    at = [iter(stages) for _ in range(NCH)]
+    for j in ORDER:
+        next(at[j])(j)
 
     for o in range(1, NX):
         xd = xat(o)
@@ -412,7 +440,7 @@
     CAP = hidden_grad.shape[1]
     LANES = DQ + META
     half_x = NX // 2
-    NCH = NX // CPC
+    NCH = len(CHUNKS)
     hbm = pl.BlockSpec(memory_space=pltpu.HBM)
     dma = pltpu.SemaphoreType.DMA
     return pl.pallas_call(
@@ -427,21 +455,21 @@
             pltpu.VMEM((NX, TD, LANES), BF),
             pltpu.VMEM((NX, TD, LANES), BF),
             pltpu.VMEM((NX, NZ, CORES, TD, LANES), BF),
-            pltpu.VMEM((NCH, NY, CPC, CAP2, DQ), BF),
-            pltpu.VMEM((NCH, NY, CPC, CAP2, DQ), BF),
+            pltpu.VMEM((NX * NY, CAP2, DQ), BF),
+            pltpu.VMEM((NX * NY, CAP2, DQ), BF),
             pltpu.VMEM((NX, DQ, 2 * HQ), BF),
             pltpu.VMEM((CAP, HQ), BF),
             pltpu.VMEM((2, half_x, CAP, 2 * HQ), BF),
             pltpu.VMEM((2, half_x, CAP, 2 * HQ), BF),
             pltpu.VMEM((NX, CAP, 2 * HQ), BF),
             pltpu.VMEM((CAP, DQ), F32),
-            pltpu.VMEM((NCH, NY, CPC, CAP2, DQ), BF),
-            pltpu.VMEM((NCH, NY, CPC, CAP2, DQ), BF),
+            pltpu.VMEM((NX * NY, CAP2, DQ), BF),
+            pltpu.VMEM((NX * NY, CAP2, DQ), BF),
             pltpu.VMEM((NX, NY * CAP2, NG * TD), BF),
-            pltpu.VMEM((NCH, NZ, CORES, CPC, TD, DQ), BF),
-            pltpu.VMEM((NCH, NZ, CPC, TD, DQ), BF),
-            pltpu.VMEM((NCH, NZ, CPC, TD, DQ), BF),
-            pltpu.VMEM((NCH, NZ, CPC, TD, DQ), BF),
+            pltpu.VMEM((NX * NZ * CORES, TD, DQ), BF),
+            pltpu.VMEM((NX * NZ, TD, DQ), BF),
+            pltpu.VMEM((NX * NZ, TD, DQ), BF),
+            pltpu.VMEM((NX * NZ, TD, DQ), BF),
             pltpu.VMEM((NX, TD, DQ), BF),
             pltpu.VMEM((NX, TD, DQ), BF),
             dma((4,)),

time: 132 us -> 120 us (0.909)
  Pallas kernels: 125 us -> 119 us
  local copies, waits for them, and re-layouts: 6.08 us -> 1.45 us
    pallas_call x1, Pallas kernels: 125 us -> 119 us  [shards(): pl.pallas_call(functools.partial(kernel, (NX, NY, NZ)), out_shape=jax.Sha...]
    unnamed x13 -> x1, local copies, waits for them, and re-layouts: 6.08 us -> 1.45 us
where the time goes in v3:
time: 120 us
  Pallas kernels  119 us (99%)
  local copies, waits for them, and re-layouts  1.45 us (1%)
    pallas_call x1, Pallas kernels, shards(): pl.pallas_call(functools.partial(kernel, (NX, NY, NZ)), out_shape=jax.Sha...  119 us

profile of v3, /device:TPU:1, one launch (start us, length us, event | category | flops | bytes accessed | tf_op | source)
XLA Modules:
  0.0 120.3 jit_solution(9205607654211042962)
XLA Ops:
  0.0 118.8 %shard_map.64 = bf16[8,3584]{1,0:T(8,128)(2,1)} custom-call(bf16[8,3584]{1,0:T(8,128)(2,1)} %tokens.1, s32[8,8]{1,0:T(8,128)} %ids.1, s32[8,8]{1,0:T(8,128)} %slots.1, bf16[448,1024]{1,0:T(8,128)(2,1)} %bitcast.3, bf16[448,1024]{1,0:T(8,128)(2,1)} %bitcast.4, bf16[512,128]{1,0:T(8,128)(2,1)} %bitcast.5), custom_call_target="tpu_custom_call" | custom-call | tf_op jit(solution)/shard_map/pallas_call | solution.py:446
  118.8 1.4 %copy.8 = bf16[8,3584]{1,0:T(8,128)(2,1)} copy(bf16[8,3584]{1,0:T(8,128)(2,1)} %shard_map.64) | data formatting | bytes 114688

commit v4 on v3

--- a/solution.py
+++ b/solution.py
@@ -16,9 +16,10 @@
 CAP2 = 8
 META = 64
 CHUNKS = (2, 2, 2, 2)
+AHEAD = 2
 ORDER = (
-    0, 0, 1, 0, 1, 0, 2, 0, 1, 2, 1, 0, 3, 2, 3, 1, 0, 2, 1, 3, 0, 2, 3, 1, 0, 2, 3, 1, 0, 2, 3,
-    0, 1, 2, 3, 0, 1, 2, 0, 3, 1, 2, 3, 2, 0, 1, 3, 1, 3, 2, 2, 1, 3, 3, 2, 3,
+    0, 1, 0, 1, 2, 3, 2, 0, 3, 1, 0, 1, 2, 0, 3, 1, 2, 3, 0, 1, 2, 3, 0, 1, 2, 3, 0, 1, 2, 3, 0,
+    1, 2, 3, 0, 1, 2, 0, 3, 1, 2, 3, 2, 0, 3, 1, 0, 1, 2, 3, 2, 3, 0, 1, 2, 3,
 )
 VMEM_BYTES = 62 * 1024 * 1024
 
@@ -204,7 +205,8 @@
         for o in range(1, NZ):
             start(z_copy(o, j, z, zat(o)))
 
-    z_send(0)
+    for j in range(AHEAD):
+        z_send(j)
     g_buf[:, pl.ds(z, 1), pl.ds(c, 1)] = a_buf[...].reshape(NX, 1, 1, TD, LANES)
 
     def core_copy(j, core):
@@ -215,8 +217,8 @@
         for o in range(1, NZ):
             z_copy(o, j, zat(-o), zat(-o)).wait_recv()
         start(core_copy(j, c))
-        if j + 1 < NCH:
-            z_send(j + 1)
+        if j + AHEAD < NCH:
+            z_send(j + AHEAD)
 
     pick_row = lax.broadcasted_iota(jnp.int32, (8, 128), 0)
     pick_lane = lax.broadcasted_iota(jnp.int32, (8, 128), 1) - (128 - META)
@@ -401,12 +403,20 @@
             q_buf[first[j] * NZ + o * CHUNKS[j] : first[j] * NZ + (o + 1) * CHUNKS[j]] = pair_sum(j, zd).astype(BF)
             start(sum_copy(o, j, zd))
 
+    def out_copy(dst, src):
+        return remote(o_buf.at[dst], f_buf.at[src], x2.at[0, dst], x2.at[1, src], at_x(dst))
+
     def sum_stage(j):
         total = pair_sum(j, z)
         for o in range(1, NZ):
             sum_copy(o, j, zat(-o)).wait_recv()
             total = total + zb[first[j] * NZ + o * CHUNKS[j] : first[j] * NZ + (o + 1) * CHUNKS[j]].astype(F32)
         o_buf[first[j] : first[j] + CHUNKS[j]] = total.astype(BF)
+        for col in range(first[j], first[j] + CHUNKS[j]):
+
+            @pl.when(x != col)
+            def _():
+                out_copy(col, x).start()
 
     stages = [gather_stage, pick_stage]
     stages += [functools.partial(rs_stage, k) for k in range(half_x)]
@@ -417,13 +427,10 @@
     for j in ORDER:
         next(at[j])(j)
 
-    for o in range(1, NX):
-        xd = xat(o)
-        start(remote(o_buf.at[xd], f_buf.at[x], x2.at[0, o], x2.at[1, o], at_x(xd)))
     f_buf[pl.ds(x, 1)] = o_buf[pl.ds(x, 1)]
     for o in range(1, NX):
-        xs = xat(-o)
-        remote(o_buf.at[xs], f_buf.at[xs], x2.at[0, o], x2.at[1, o], at_x(xs)).wait_recv()
+        out_copy(xat(-o), xat(-o)).wait_recv()
+        out_copy(xat(o), x).wait_send()
     out[...] = jnp.concatenate([f_buf[d].astype(F32) for d in range(NX)], axis=1).astype(BF)
     for copy in sends:
         copy.wait_send()

time: 120 us -> 116 us (0.967); the launches traced: 120 us -> 114 us
  Pallas kernels: 119 us -> 113 us
    pallas_call x1, Pallas kernels: 119 us -> 113 us  [shards(): pl.pallas_call(functools.partial(kernel, (NX, NY, NZ)), out_shape=jax.Sha...]
where the time goes in v4:
time: 116 us; the launch traced here: 114 us
  Pallas kernels  113 us (97%)
  local copies, waits for them, and re-layouts  1.45 us (1%)
    pallas_call x1, Pallas kernels, shards(): pl.pallas_call(functools.partial(kernel, (NX, NY, NZ)), out_shape=jax.Sha...  113 us

profile of v4, /device:TPU:1, one launch (start us, length us, event | category | flops | bytes accessed | tf_op | source)
XLA Modules:
  0.0 114.2 jit_solution(2550382633875282467)
XLA Ops:
  0.0 112.7 %shard_map.64 = bf16[8,3584]{1,0:T(8,128)(2,1)} custom-call(bf16[8,3584]{1,0:T(8,128)(2,1)} %tokens.1, s32[8,8]{1,0:T(8,128)} %ids.1, s32[8,8]{1,0:T(8,128)} %slots.1, bf16[448,1024]{1,0:T(8,128)(2,1)} %bitcast.3, bf16[448,1024]{1,0:T(8,128)(2,1)} %bitcast.4, bf16[512,128]{1,0:T(8,128)(2,1)} %bitcast.5), custom_call_target="tpu_custom_call" | custom-call | tf_op jit(solution)/shard_map/pallas_call | solution.py:453
  112.7 1.4 %copy.8 = bf16[8,3584]{1,0:T(8,128)(2,1)} copy(bf16[8,3584]{1,0:T(8,128)(2,1)} %shard_map.64) | data formatting | bytes 114688
